TPU v7x, 1024 devices: a whole 4x8x16 slice. The times are simulated.
1024 devices in a mesh: replica: 4 (over z_lo), fsdp: 256 (over z_hi, x, y, core).
Axes of the slice: x: 4, y: 8, z: 16 (z_hi: 4, z_lo: 4; z = z_hi * 4 + z_lo), core: 2. Of those that a mesh axis runs over, the one named last changes fastest.
Arguments:
- tokens: bfloat16 [196608, 8192], P(('replica', 'fsdp')), may hold values from -6 to 6
- outer_base: float32 [8192, 256], P('fsdp'), may hold values from -5 to 5
- outer_momentum: float32 [8192, 256], P('fsdp'), may hold values from -3 to 3
- replica_weights: bfloat16 [4, 8192, 256], P('replica', 'fsdp'), may hold values from -8 to 8
- block_exponent: int32 [4, 8192, 2], P('replica', 'fsdp'), may hold values from -11 to -4
Outputs:
- key_value: bfloat16 [196608, 256], P(('replica', 'fsdp'))
- next_base: float32 [8192, 256], P('fsdp', 'replica')
- next_momentum: float32 [8192, 256], P('fsdp', 'replica')
All inputs are finite; a program needn't handle non-finite values.
Results may differ from a plain program's by a relative error of at most 0.007.
Values may be sent and summed in bfloat16 or wider, within the bound.
A program may use at most 32 MiB of HBM per device.

v0:
```python
import jax
import jax.numpy as jnp
from jax import lax
from jax.sharding import PartitionSpec as P

D = 8192
BLOCK = 128


code_limit = 448.0
momentum_rate = 0.9
outer_rate = 0.7


def body(tokens, outer_base, outer_momentum, replica_weights, block_exponent):
    row_count, width = outer_base.shape
    difference = outer_base - replica_weights[0].astype(jnp.float32)
    blocked = difference.reshape(row_count, width // BLOCK, BLOCK)
    powers = block_exponent[0].astype(jnp.float32)[..., None]
    encoded = jnp.clip(blocked * jnp.exp2(-powers), -code_limit, code_limit).astype(jnp.bfloat16)
    encoded = lax.optimization_barrier(encoded)
    decoded = (encoded.astype(jnp.float32) * jnp.exp2(powers)).reshape(row_count, width)
    replicas = lax.axis_size("replica")
    share_width = width // replicas
    column_offset = lax.axis_index("replica") * share_width
    summed = lax.psum(decoded.astype(jnp.bfloat16), "replica").astype(jnp.float32)
    average = summed / replicas
    momentum_whole = momentum_rate * outer_momentum + average
    base_whole = outer_base - outer_rate * (average + momentum_rate * momentum_whole)
    next_momentum = lax.dynamic_slice_in_dim(momentum_whole, column_offset, share_width, 1)
    next_base = lax.dynamic_slice_in_dim(base_whole, column_offset, share_width, 1)
    weights = base_whole.astype(jnp.bfloat16)
    projected = jnp.dot(
        tokens,
        lax.all_gather(weights, "fsdp", axis=0, tiled=True),
        preferred_element_type=jnp.float32,
    )
    key_value = (projected * D ** (-0.5)).astype(jnp.bfloat16)
    return (key_value, next_base, next_momentum)


def solution(mesh):
    return jax.shard_map(
        body,
        mesh=mesh,
        in_specs=(
            P(("replica", "fsdp"), None),
            P("fsdp", None),
            P("fsdp", None),
            P("replica", "fsdp", None),
            P("replica", "fsdp", None),
        ),
        out_specs=(P(("replica", "fsdp"), None), P("fsdp", "replica"), P("fsdp", "replica")),
        check_vma=False,
    )
```

profile of v0, /device:TPU:1, one launch (start us, length us, event | category | flops | bytes accessed | tf_op | source)
XLA Modules:
  0.0 207.3 jit_solution(2322722859553789587)
XLA Ops:
  7.2 0.0 copy-start
  7.2 0.0 all-gather.2.cloned.1.call-start
  7.2 0.8 exponential_bitcast_fusion
  8.1 0.1 copy.8
  8.2 0.8 convert_subtract_fusion
  8.9 0.1 clamp_convert_fusion
  9.1 0.1 copy.9
  9.1 0.1 multiply_convert_fusion
  9.3 18.5 %psum.7 = bf16[32,256]{1,0:T(8,128)(2,1)S(1)} all-reduce(bf16[32,256]{1,0:T(8,128)(2,1)S(1)} %bitcast.16), channel_id=1, replica_groups=mesh['replica'=4,'fsdp'=256] {'replica'}, use_global_device_ids=true, to_apply=%region_0.1 | all-reduce | flops 8192 | bytes 32768 | tf_op jit(solution)/shard_map/psum | solution.py:26
  27.7 1.4 fusion.2
  29.1 0.0 all-gather.2.cloned.1.call-update
  29.1 0.7 constant_dynamic-slice_fusion
  29.8 166.8 %all-gather.2.cloned.1.call-done = bf16[8192,256]{1,0:T(8,128)(2,1)} async-done(((bf16[32,256]{1,0:T(8,128)(2,1)}), bf16[8192,256]{1,0:T(8,128)(2,1)}) %all-gather.2.cloned.1.call-update) | async-done | bytes 4194320 | tf_op jit(solution)/shard_map/all_gather | solution.py:35
  196.6 0.0 copy-done
  196.6 3.8 %fusion.1 = bf16[192,256]{1,0:T(8,128)(2,1)} fusion(bf16[192,8192]{1,0:T(8,128)(2,1)S(1)} %copy-done, bf16[8192,256]{1,0:T(8,128)(2,1)} %all-gather.2.cloned.1.call-done), kind=kOutput, calls=%fused_computation.2 | convolution fusion | flops 805404672 | bytes 7438336 | tf_op jit(solution)/shard_map/dot_general | solution.py:33
  (2 shorter events, 0.0 us)
Async XLA Ops:
  7.2 189.5 %copy-start = (bf16[192,8192]{1,0:T(8,128)(2,1)S(1)}, bf16[192,8192]{1,0:T(8,128)(2,1)}, u32[]{:S(2)}) copy-start(bf16[192,8192]{1,0:T(8,128)(2,1)} %param.5) | copy-start | bytes 9437188
  7.2 189.4 %all-gather.2.cloned.1.call-start = ((), (), s32[]{:S(2)}) async-start(), calls=%async_computation | async-start | bytes 4210688 | tf_op jit(solution)/shard_map/all_gather | solution.py:35
Sparse Core Ops, SparseCore 0:
  29.3 167.3 all-gather.1
where the time goes:
time: 208 us; the launch traced here: 207 us
  waiting for transfers between devices  167 us (80%)
  blocking collectives  18.5 us (9%)
  between operations  14.1 us (7%)
  matrix products  3.81 us (2%)
  other arithmetic  3.19 us (2%)
    all_gather x1, waiting for transfers between devices, body(): lax.all_gather(weights, 'fsdp', axis=0, tiled=True)  167 us
    psum x1, blocking collectives, body(): lax.psum(decoded.astype(jnp.bfloat16), 'replica').astype(jnp.float32)  18.5 us
  transfers between devices with their start and end apart: 1, of which 1 were waited for; matrix products, arithmetic and copies ran while one was open for 0% of the time, Pallas kernels for 0%

commit v1 on v0

v1 whole, which is shorter than its diff:
```python
import functools

import jax
import jax.numpy as jnp
from jax import lax
from jax.experimental import pallas as pl
from jax.experimental.pallas import tpu as pltpu
from jax.sharding import PartitionSpec as P

MESH = pl.DeviceIdType.MESH
BLOCK = 128
CODE_LIMIT = 448.0
MOMENTUM_RATE = 0.9
OUTER_RATE = 0.7
LOW_EXP, HIGH_EXP = -11, -4

NX, NY, NH, NR = 4, 8, 4, 4


def place():
    r, f = lax.axis_index("replica"), lax.axis_index("fsdp")
    c, y = f % 2, (f // 2) % NY
    x, zh = (f // (2 * NY)) % NX, f // (2 * NY * NX)
    return x, y, zh, r, c


def kernel(
    tok_hbm, base_ref, mom_ref, rep_ref, exp_ref,
    kv_ref, nb_ref, nm_ref,
    tok, dec, part, w, acc, half_b,
    tok_sem, s0, r0, sh, rh, s1, r1, s2, r2, s3, r3, sc, rc,
):
    x, y, zh, r, c = place()

    def dev(x, y, zh, r, c):
        return (r, ((zh * NX + x) * NY + y) * 2 + c)

    def to_r(d):
        return dev(x, y, zh, (r + d) % NR, c)

    def to_h(d):
        return dev(x, y, (zh + d) % NH, r, c)

    def to_y(d):
        return dev(x, (y + d) % NY, zh, r, c)

    def to_x(d):
        return dev((x + d) % NX, y, zh, r, c)

    def to_z(d):
        z = (zh * NR + r + d + NR * NH) % (NR * NH)
        return dev(x, y, z // NR, z % NR, c)

    other = dev(x, y, zh, r, 1 - c)

    def pick(flag, a, b):
        return tuple(jnp.where(flag, i, j) for i, j in zip(a, b))

    tok_copy = pltpu.make_async_copy(tok_hbm, tok, tok_sem)
    tok_copy.start()

    bar = pltpu.get_barrier_semaphore()
    greet = [to_r(d) for d in range(1, NR)] + [to_h(d) for d in range(1, NH)]
    greet += [to_y(d) for d in range(1, NY)] + [to_x(d) for d in (1, 2, 3)]
    greet += [to_z(d) for d in (1, -1, -2)] + [other]
    for who in greet:
        pl.semaphore_signal(bar, inc=1, device_id=who, device_id_type=MESH)

    exps = exp_ref[0]
    up = jnp.zeros(exps.shape, jnp.float32)
    down = jnp.zeros(exps.shape, jnp.float32)
    for e in range(LOW_EXP, HIGH_EXP + 1):
        up = jnp.where(exps == e, 2.0**-e, up)
        down = jnp.where(exps == e, 2.0**e, down)
    for v in range(2):
        cols = slice(v * BLOCK, (v + 1) * BLOCK)
        diff = base_ref[:, cols] - rep_ref[0, :, cols].astype(jnp.float32)
        code = jnp.clip(diff * up[:, v : v + 1], -CODE_LIMIT, CODE_LIMIT)
        code = code.astype(jnp.bfloat16).astype(jnp.float32)
        dec[v] = (code * down[:, v : v + 1]).astype(jnp.bfloat16)

    pl.semaphore_wait(bar, len(greet))

    pending = []

    def send(src, dst, ss, rs, who):
        cp = pltpu.make_async_remote_copy(
            src_ref=src, dst_ref=dst, send_sem=ss, recv_sem=rs, device_id=who, device_id_type=MESH
        )
        cp.start()
        pending.append(cp)

    def arrive(dst, ss, rs):
        pltpu.make_async_remote_copy(
            src_ref=dst, dst_ref=dst, send_sem=ss, recv_sem=rs, device_id=other, device_id_type=MESH
        ).wait_recv()

    for d in range(1, NR):
        p = (r + d) % NR
        send(dec.at[p // 2], part.at[NR - d], s0.at[d], r0.at[NR - d], to_r(d))
    part[0] = dec[r // 2]
    for d in range(1, NR):
        arrive(part.at[d], s0.at[d], r0.at[d])
    total = part[0].astype(jnp.float32)
    for d in range(1, NR):
        total = total + part[d].astype(jnp.float32)
    average = total / NR
    mine = pl.ds(pl.multiple_of((r // 2) * BLOCK, BLOCK), BLOCK)
    new_mom = MOMENTUM_RATE * mom_ref[:, mine] + average
    new_base = base_ref[:, mine] - OUTER_RATE * (average + MOMENTUM_RATE * new_mom)
    odd = (r % 2) == 1
    piece = jnp.where(odd, new_base[16:], new_base[:16]).astype(jnp.bfloat16)

    def flip(h):
        return (h + c) % 2

    def st(h):
        return jnp.where(flip(h) == 0, x, r), jnp.where(flip(h) == 0, r, x)

    s_own, t_own = st(zh)
    w[zh, c, s_own, t_own, y] = piece

    def hs(d):
        return (zh + d) % NH

    for d in (2, 1, 3):
        cell = w.at[zh, c, s_own, t_own, y]
        send(cell, cell, sh.at[d], rh.at[NH - d], to_h(d))

    def run_wait(d):
        h = hs(d)
        s, t = st(h)
        arrive(w.at[h, c, s, t, y], sh.at[d], rh.at[d])

    def y_send(d):
        h = hs(d)
        s, t = st(h)
        cell = w.at[h, c, s, t, y]
        for e in (4, 3, 5, 2, 6, 1, 7):
            send(cell, cell, s1.at[d, e], r1.at[d, NY - e], to_y(e))

    def y_wait(d):
        h = hs(d)
        s, t = st(h)
        for e in range(1, NY):
            arrive(w.at[h, c, s, t, (y + e) % NY], s1.at[d, e], r1.at[d, e])

    def t_send(d):
        h = hs(d)
        s, t = st(h)
        row = w.at[h, c, s, t]
        for e in (2, 1, 3):
            who = pick(flip(h) == 0, to_z(e if e < 3 else -1), to_x(e))
            send(row, row, s2.at[h, e], r2.at[h, 4 - e], who)

    def t_wait(d):
        h = hs(d)
        s, t = st(h)
        for e in (1, 3, 2):
            arrive(w.at[h, c, s, (t + e) % 4], s2.at[h, e], r2.at[h, e])

    def core_send(h, block, i):
        send(block, block, sc.at[h, i], rc.at[h, i], other)

    def s_peer(h, e):
        return pick(flip(h) == 0, to_x(e), to_z(e if e < 3 else -1))

    def s_send(d):
        h = hs(d)
        s, t = st(h)
        block = w.at[h, c, s]
        for e in (1, 3):
            send(block, block, s3.at[h, e], r3.at[h, 4 - e], s_peer(h, e))
        core_send(h, block, 0)

    def s_forward(d):
        h = hs(d)
        s, t = st(h)
        for e, lo in ((3, 0), (1, 2)):
            block = w.at[h, c, (s + e) % 4]
            arrive(block, s3.at[h, e], r3.at[h, e])
            piece = block.at[pl.ds(lo, 2)]
            send(piece, piece, s3.at[h, 0 if e == 3 else 2], r3.at[h, 0 if e == 3 else 2], s_peer(h, 4 - e))
            core_send(h, block, e)

    def s_wait(d):
        h = hs(d)
        s, t = st(h)
        for k, lo in ((0, 0), (2, 2)):
            piece = w.at[h, c, (s + 2) % 4, pl.ds(lo, 2)]
            arrive(piece, s3.at[h, k], r3.at[h, k])
            core_send(h, piece, 2 if k == 0 else 4)

    def core_wait(d):
        h = hs(d)
        o = 1 - c
        so = jnp.where(flip(h) == 0, r, x)
        arrive(w.at[h, o, so], sc.at[h, 0], rc.at[h, 0])
        for e in (3, 1):
            arrive(w.at[h, o, (so + e) % 4], sc.at[h, e], rc.at[h, e])
        for i, lo in ((2, 0), (4, 2)):
            arrive(w.at[h, o, (so + 2) % 4, pl.ds(lo, 2)], sc.at[h, i], rc.at[h, i])

    def multiply(d, first):
        h = hs(d)
        depth = NY * 64

        def step(i, total):
            tiles = {}
            for cc in range(2):
                for p in range(NR):
                    turned = (h + cc) % 2 == 1
                    si, ti = jnp.where(turned, p, i), jnp.where(turned, i, p)
                    for yy in range(NY):
                        tiles[yy, cc, p] = w[h, cc, si, ti, yy]
            rows = [
                jnp.concatenate([tiles[yy, cc, q], tiles[yy, cc, 2 + q]], axis=1)
                for yy in range(NY) for cc in range(2) for q in range(2)
            ]
            weights = jnp.concatenate(rows, axis=0)
            at = pl.multiple_of((h * NX + i) * depth, depth)
            acc[...] += jnp.dot(tok[:, pl.ds(at, depth)], weights, preferred_element_type=jnp.float32)
            return total

        lax.fori_loop(0, NX, step, 0)

    y_send(0)
    nm_ref[...] = jnp.where(odd, new_mom[:, 64:], new_mom[:, :64])
    nb_ref[...] = jnp.where(odd, new_base[:, 64:], new_base[:, :64])
    acc[...] = jnp.zeros_like(acc)
    for d in (1, 3):
        run_wait(d)
        y_send(d)
    y_wait(0)
    t_send(0)
    run_wait(2)
    y_send(2)
    for d in (1, 3):
        y_wait(d)
        t_send(d)
    t_wait(0)
    s_send(0)
    y_wait(2)
    t_send(2)
    for d in (1, 3, 2):
        t_wait(d)
        s_send(d)
    tok_copy.wait()
    for d in (0, 1, 3, 2):
        s_forward(d)
    for d in (0, 1, 3, 2):
        s_wait(d)
        core_wait(d)
        multiply(d, d == 0)
    kv_ref[...] = (acc[...] * (NX * NY * NH * 64) ** -0.5).astype(jnp.bfloat16)
    for cp in pending:
        cp.wait_send()


def body(tokens, outer_base, outer_momentum, replica_weights, block_exponent):
    rows, depth = tokens.shape
    local, width = outer_base.shape
    dma = pltpu.SemaphoreType.DMA
    vmem = pl.BlockSpec(memory_space=pltpu.VMEM)
    return pl.pallas_call(
        kernel,
        out_shape=(
            jax.ShapeDtypeStruct((rows, width), jnp.bfloat16),
            jax.ShapeDtypeStruct((local, width // NR), jnp.float32),
            jax.ShapeDtypeStruct((local, width // NR), jnp.float32),
        ),
        in_specs=[pl.BlockSpec(memory_space=pl.ANY)] + [vmem] * 4,
        out_specs=(vmem, vmem, vmem),
        scratch_shapes=[
            pltpu.VMEM((rows, depth), jnp.bfloat16),
            pltpu.VMEM((2, local, BLOCK), jnp.bfloat16),
            pltpu.VMEM((NR, local, BLOCK), jnp.bfloat16),
            pltpu.VMEM((NH, 2, 4, 4, NY, 16, BLOCK), jnp.bfloat16),
            pltpu.VMEM((rows, width), jnp.float32),
            pltpu.VMEM((local, BLOCK), jnp.float32),
            dma,
            dma((NR,)), dma((NR,)),
            dma((NH,)), dma((NH,)),
            dma((NH, NY)), dma((NH, NY)),
            dma((NH, 4)), dma((NH, 4)),
            dma((NH, 4)), dma((NH, 4)),
            dma((NH, 5)), dma((NH, 5)),
        ],
        compiler_params=pltpu.CompilerParams(
            collective_id=0, has_side_effects=True, vmem_limit_bytes=40 << 20
        ),
        cost_estimate=pl.CostEstimate(
            flops=2 * rows * depth * width, bytes_accessed=2 * rows * depth, transcendentals=0
        ),
        name="outer_step_project",
    )(tokens, outer_base, outer_momentum, replica_weights, block_exponent)


def solution(mesh):
    return jax.shard_map(
        body,
        mesh=mesh,
        in_specs=(
            P(("replica", "fsdp"), None),
            P("fsdp", None),
            P("fsdp", None),
            P("replica", "fsdp", None),
            P("replica", "fsdp", None),
        ),
        out_specs=(P(("replica", "fsdp"), None), P("fsdp", "replica"), P("fsdp", "replica")),
        check_vma=False,
    )
```

time: 208 us -> 70.1 us (0.34)
  waiting for transfers between devices: 167 us -> 0 us
  Pallas kernels: 0 us -> 62.3 us
  blocking collectives: 18.5 us -> 0 us
  between operations: 14.1 us -> 0.64 us
  local copies, waits for them, and re-layouts: 0.91 us -> 6.73 us
  matrix products: 3.81 us -> 0 us
  other arithmetic: 3.19 us -> 0 us
    all_gather x1 -> x0, waiting for transfers between devices: 167 us -> none  [body(): lax.all_gather(weights, 'fsdp', axis=0, tiled=True)]
    pallas_call x0 -> x1, Pallas kernels: none -> 62.3 us  [body(): pl.pallas_call(kernel, out_shape=(jax.ShapeDtypeStruct((rows, width), jnp...]
    psum x1 -> x0, blocking collectives: 18.5 us -> none  [body(): lax.psum(decoded.astype(jnp.bfloat16), 'replica').astype(jnp.float32)]
    unnamed x3 -> x12, local copies, waits for them, and re-layouts: 0.02 us -> 6.73 us
    dot_general x1 -> x0, matrix products: 3.81 us -> none  [body(): jnp.dot(tokens, lax.all_gather(weights, 'fsdp', axis=0, tiled=True), pref...]
  transfers between devices with their start and end apart: 1 -> 0, of which waited for: 1 -> 0; matrix products, arithmetic and copies ran while one was open for 0% -> 0% of each run, Pallas kernels for 0% -> 0%
where the time goes in v1:
time: 70.1 us; the launch traced here: 69.7 us
  Pallas kernels  62.3 us (89%)
  local copies, waits for them, and re-layouts  6.73 us (10%)
    pallas_call x1, Pallas kernels, body(): pl.pallas_call(kernel, out_shape=(jax.ShapeDtypeStruct((rows, width), jnp...  62.3 us
    unnamed x12, local copies, waits for them, and re-layouts  6.73 us

profile of v1, /device:TPU:1, one launch (start us, length us, event | category | flops | bytes accessed | tf_op | source)
XLA Modules:
  0.0 69.7 jit_solution(2196665451716308988)
XLA Ops:
  0.6 0.8 %copy.8.exp_ref = s32[1,32,2]{2,1,0:T(8,128)S(1)} copy(s32[1,32,2]{1,2,0:T(2,128)} %param.9) | data formatting | bytes 512 | tf_op args[4]
  1.4 0.0 copy-start
  1.4 1.9 %copy-done = bf16[192,8192]{1,0:T(8,128)(2,1)S(1)} copy-done((bf16[192,8192]{1,0:T(8,128)(2,1)S(1)}, bf16[192,8192]{1,0:T(8,128)(2,1)}, u32[]{:S(2)}) %copy-start) | copy-done | bytes 3145752
  3.3 0.0 copy-start.1
  3.3 0.8 %copy-done.1 = f32[32,256]{1,0:T(8,128)S(1)} copy-done((f32[32,256]{1,0:T(8,128)S(1)}, f32[32,256]{1,0:T(8,128)}, u32[]{:S(2)}) %copy-start.1) | copy-done | bytes 32792
  4.0 0.0 copy-start.2
  4.0 0.8 %copy-done.2 = f32[32,256]{1,0:T(8,128)S(1)} copy-done((f32[32,256]{1,0:T(8,128)S(1)}, f32[32,256]{1,0:T(8,128)}, u32[]{:S(2)}) %copy-start.2) | copy-done | bytes 32792
  4.8 0.0 copy-start.3
  4.8 0.7 %copy-done.3 = bf16[1,32,256]{2,1,0:T(8,128)(2,1)S(1)} copy-done((bf16[1,32,256]{2,1,0:T(8,128)(2,1)S(1)}, bf16[1,32,256]{2,1,0:T(8,128)(2,1)}, u32[]{:S(2)}) %copy-start.3) | copy-done | bytes 16408
  5.5 62.3 %outer_step_project.1 = (bf16[192,256]{1,0:T(8,128)(2,1)S(1)}, f32[32,64]{1,0:T(8,128)S(1)}, f32[32,64]{1,0:T(8,128)S(1)}) custom-call(bf16[192,8192]{1,0:T(8,128)(2,1)S(1)} %copy-done, f32[32,256]{1,0:T(8,128)S(1)} %copy-done.1, f32[32,256]{1,0:T(8,128)S(1)} %copy-done.2, bf16[1,32,256]{2,1,0:T(8,128)(2,1)S(1)} %copy-done.3, s32[1,32,2]{2,1,0:T(8,128)S(1)} %copy.8.exp_ref), custom_call_target="tpu_custom_call" | custom-call | flops 805306368 | bytes 3145728 | tf_op jit(solution)/shard_map/outer_step_project/pallas_call | solution.py:265
  67.9 0.6 copy.12
  68.5 0.6 copy.13
  69.1 0.6 copy.14
Async XLA Ops:
  1.4 1.9 %copy-start = (bf16[192,8192]{1,0:T(8,128)(2,1)S(1)}, bf16[192,8192]{1,0:T(8,128)(2,1)}, u32[]{:S(2)}) copy-start(bf16[192,8192]{1,0:T(8,128)(2,1)} %tok_hbm.1) | copy-start | bytes 9437188
  3.3 0.8 %copy-start.1 = (f32[32,256]{1,0:T(8,128)S(1)}, f32[32,256]{1,0:T(8,128)}, u32[]{:S(2)}) copy-start(f32[32,256]{1,0:T(8,128)} %base_ref.1) | copy-start | bytes 98308
  4.0 0.8 %copy-start.2 = (f32[32,256]{1,0:T(8,128)S(1)}, f32[32,256]{1,0:T(8,128)}, u32[]{:S(2)}) copy-start(f32[32,256]{1,0:T(8,128)} %mom_ref.1) | copy-start | bytes 98308
  4.8 0.7 %copy-start.3 = (bf16[1,32,256]{2,1,0:T(8,128)(2,1)S(1)}, bf16[1,32,256]{2,1,0:T(8,128)(2,1)}, u32[]{:S(2)}) copy-start(bf16[1,32,256]{2,1,0:T(8,128)(2,1)} %rep_ref.1) | copy-start | bytes 49156

commit v2 on v0

v2 whole, which is shorter than its diff:
```python
import functools

import jax
import jax.numpy as jnp
from jax import lax
from jax.experimental import pallas as pl
from jax.experimental.pallas import tpu as pltpu
from jax.sharding import PartitionSpec as P

MESH = pl.DeviceIdType.MESH
BLOCK = 128
CODE_LIMIT = 448.0
MOMENTUM_RATE = 0.9
OUTER_RATE = 0.7
LOW_EXP, HIGH_EXP = -11, -4

NX, NY, NH, NR = 4, 8, 4, 4


def place():
    r, f = lax.axis_index("replica"), lax.axis_index("fsdp")
    c, y = f % 2, (f // 2) % NY
    x, zh = (f // (2 * NY)) % NX, f // (2 * NY * NX)
    return x, y, zh, r, c


def kernel(
    tok_hbm, base_hbm, mom_hbm, rep_hbm, exp_hbm,
    kv_ref, nb_ref, nm_ref,
    tok, base_ref, mom_ref, rep_ref, exp_ref, turn, dec, part, w, acc,
    in_sem, s0, r0, sh, rh, s1, r1, s3, r3, rest3, s4, r4, sc, rc, ready,
):
    x, y, zh, r, c = place()
    z = zh * NR + r
    nz = NR * NH

    def dev(x, y, zh, r, c):
        return (r, ((zh * NX + x) * NY + y) * 2 + c)

    def to_r(d):
        return dev(x, y, zh, (r + d) % NR, c)

    def to_y(d):
        return dev(x, (y + d) % NY, zh, r, c)

    def to_x(d):
        return dev((x + d) % NX, y, zh, r, c)

    def at_z(z):
        return dev(x, y, z // NR, z % NR, c)

    other = dev(x, y, zh, r, 1 - c)

    def signal(sem, who):
        pl.semaphore_signal(sem, inc=1, device_id=who, device_id_type=MESH)

    loads = [
        pltpu.make_async_copy(src, dst, in_sem.at[i])
        for i, (src, dst) in enumerate(
            ((base_hbm, base_ref), (rep_hbm, rep_ref), (exp_hbm, exp_ref), (mom_hbm, mom_ref), (tok_hbm, tok))
        )
    ]
    for load in loads:
        load.start()

    edge = (r == 0) | (r == NR - 1)
    way = jnp.where(r == 0, -1, 1)

    def target(o):
        return (z + way * o + nz) % nz

    low, high, far = (zh + NH - 1) % NH, (zh + 1) % NH, (zh + 2) % NH
    upward = r < 2
    sources = (
        (low, low * NR + NR - 1, r + 1),
        (high, high * NR, NR - r),
        (far, jnp.where(upward, far * NR + NR - 1, far * NR), jnp.where(upward, 5 + r, 8 - r)),
    )

    bar = pltpu.get_barrier_semaphore()
    inside = [to_r(d) for d in range(1, NR)] + [to_y(d) for d in range(1, NY)]
    inside += [to_x(1), to_x(-1 + NX), other]
    for who in inside:
        signal(bar, who)
    for h, src, _ in sources:
        pl.when(h > zh)(functools.partial(signal, bar, at_z(src)))
    slots = range(1, 7)
    for o in slots:
        pl.when(edge & (target(o) // NR > zh))(functools.partial(signal, bar, at_z(target(o))))

    for load in loads[:4]:
        load.wait()
    exps = exp_ref[0]
    up = jnp.zeros(exps.shape, jnp.float32)
    down = jnp.zeros(exps.shape, jnp.float32)
    for e in range(LOW_EXP, HIGH_EXP + 1):
        up = jnp.where(exps == e, 2.0**-e, up)
        down = jnp.where(exps == e, 2.0**e, down)
    local = exps.shape[1]
    turn[...] = jnp.zeros_like(turn)
    turn[0:2, :local] = up
    turn[2:4, :local] = down
    scales = turn[...].T
    up, down = scales[:local, 0:2], scales[:local, 2:4]
    for v in range(2):
        cols = slice(v * BLOCK, (v + 1) * BLOCK)
        diff = base_ref[:, cols] - rep_ref[0, :, cols].astype(jnp.float32)
        code = jnp.clip(diff * up[:, v : v + 1], -CODE_LIMIT, CODE_LIMIT)
        code = code.astype(jnp.bfloat16).astype(jnp.float32)
        dec[:, cols] = (code * down[:, v : v + 1]).astype(jnp.bfloat16)

    below = sum((edge & (target(o) // NR < zh)).astype(jnp.int32) for o in slots)
    below += sum((h < zh).astype(jnp.int32) for h, _, _ in sources)
    pl.semaphore_wait(bar, len(inside) + below)

    def copy(src, dst, ss, rs, who):
        return pltpu.make_async_remote_copy(
            src_ref=src, dst_ref=dst, send_sem=ss, recv_sem=rs, device_id=who, device_id_type=MESH
        )

    def send(ref, ss, rs, who):
        copy(ref, ref, ss, rs, who).start()

    def arrive(ref, rs):
        copy(ref, ref, in_sem.at[0], rs, other).wait_recv()

    def left(ref, ss):
        copy(ref, ref, ss, in_sem.at[0], other).wait_send()

    for d in (3, 1, 2):
        copy(dec, part.at[NR - d], s0.at[d], r0.at[NR - d], to_r(d)).start()
    for h, src, o in sources:
        pl.when(h < zh)(functools.partial(signal, ready.at[o], at_z(src)))
    total = dec[...].astype(jnp.float32)
    for d in (1, 3, 2):
        arrive(part.at[d], r0.at[d])
        total = total + part[d].astype(jnp.float32)
    average = total / NR
    new_mom = MOMENTUM_RATE * mom_ref[...] + average
    new_base = base_ref[...] - OUTER_RATE * (average + MOMENTUM_RATE * new_mom)
    own = w.at[zh, x, y, c]
    own[...] = new_base.astype(jnp.bfloat16)

    across = NH - 1 - zh
    order = (zh, zh + 1 - 2 * (zh % 2), across, across + 1 - 2 * (across % 2))

    def push(o, higher):
        run = target(o) // NR

        @pl.when(edge & ((run > zh) if higher else (run < zh)))
        def _():
            if higher:
                pl.semaphore_wait(ready.at[o], 1)
            send(own, sh.at[o], rh.at[zh], at_z(target(o)))

    def push_up():
        for o in (4, 3, 2, 1, 6, 5):
            push(o, True)

    def cell(k, dx, e):
        return w.at[order[k], (x + dx) % NX, (y + e) % NY, c]

    near = (1, 7, 2, 6, 3, 5, 4)
    from_left, from_right = (0, 7, 6, 5), (1, 2, 3, 4)

    def x_send(k, e):
        mine = cell(k, 0, e)
        for d in (1, 3):
            on = from_left if d == 1 else from_right
            sem = r3.at[k, e] if e in on else rest3.at[k, 4 - d]
            send(mine, s3.at[k], sem, to_x(d))

    def launch(k):
        if k > 0:
            arrive(cell(k, 0, 0), rh.at[order[k]])
        mine = cell(k, 0, 0)
        for e in (4, 3, 5, 2, 6, 1, 7):
            send(mine, s1.at[k], r1.at[k, NY - e], to_y(e))
        x_send(k, 0)

    def take(k, e):
        arrive(cell(k, 0, e), r1.at[k, e])
        x_send(k, e)

    def forward(k, e):
        d = 3 if e in from_left else 1
        block = cell(k, d, e)
        arrive(block, r3.at[k, e])
        send(block, s4.at[k], r4.at[k, e], to_x(4 - d))

    def core_send(k, block, i):
        send(block, sc.at[k], rc.at[k, i], other)

    def own_block(k):
        core_send(k, w.at[order[k], x, :, c], 0)

    def side_block(k, d):
        block = w.at[order[k], (x + d) % NX, :, c]
        arrive(block.at[pl.ds(0, 4)], rest3.at[k, d])
        core_send(k, block, d)

    def far_cell(k, e):
        block = cell(k, 2, e)
        arrive(block, r4.at[k, e])
        core_send(k, block, 2)

    o = 1 - c
    depth = NY * 64

    def dot(h, xx):
        at = pl.multiple_of((h * NX + xx) * depth, depth)
        weights = w[h, xx].reshape(depth, weights_width)
        acc[...] += jnp.dot(tok[:, pl.ds(at, depth)], weights, preferred_element_type=jnp.float32)

    weights_width = w.shape[-1]

    def multiply(k):
        h = order[k]
        for d in (0, 3, 1):
            arrive(w.at[h, (x + d) % NX, :, o], rc.at[k, d])

        @pl.loop(0, 3)
        def _(i):
            dot(h, (x + NX - 1 + i) % NX)

    def multiply_far(k):
        h = order[k]
        xx = (x + 2) % NX
        arrive(w.at[h, xx, :, o], rc.at[k, 2])
        dot(h, xx)

    def write_step():
        for q in range(NR):
            cols = slice(q * 64, (q + 1) * 64)

            @pl.when(r == q)
            def _():
                nm_ref[...] = new_mom[:, cols]
                nb_ref[...] = new_base[:, cols]

        acc[...] = jnp.zeros_like(acc)

    def drain(k):
        left(w.at[0, 0, pl.ds(0, 7), 0], s1.at[k])
        left(w.at[0, 0], s3.at[k])
        left(w.at[0, 0, :, 0], s4.at[k])
        left(w.at[0, :, :, 0], sc.at[k])

    forwards = (0, 1, 7, 2, 6, 3, 5, 4)

    for o_ in (4, 3, 2, 1, 6, 5):
        push(o_, False)
    launch(0)
    pl.when(zh > 0)(push_up)
    write_step()
    for e in near:
        take(0, e)
    for e in forwards:
        forward(0, e)
    pl.when(zh == 0)(push_up)
    launch(1)
    own_block(0)
    side_block(0, 3)
    side_block(0, 1)
    for e in near:
        take(1, e)
    loads[4].wait()
    for e in forwards:
        far_cell(0, e)
    multiply(0)
    launch(2)
    launch(3)
    for e in forwards:
        forward(1, e)
    own_block(1)
    side_block(1, 3)
    side_block(1, 1)
    multiply_far(0)
    for e in near:
        take(2, e)
        take(3, e)
    for e in forwards:
        far_cell(1, e)
    own_block(2)
    own_block(3)
    for e in forwards:
        forward(2, e)
        forward(3, e)
    side_block(2, 3)
    side_block(2, 1)
    side_block(3, 3)
    side_block(3, 1)
    multiply(1)
    multiply_far(1)
    drain(0)
    drain(1)
    for e in forwards:
        far_cell(2, e)
        far_cell(3, e)
    multiply(2)
    multiply(3)
    multiply_far(2)
    multiply_far(3)
    kv_ref[...] = (acc[...] * (NX * NY * NH * 64) ** -0.5).astype(jnp.bfloat16)
    for d in range(1, NR):
        left(dec, s0.at[d])
    for o_ in slots:
        pl.when(edge)(functools.partial(left, own, sh.at[o_]))
    drain(2)
    drain(3)


def finish(kv_in, nb_in, nm_in, kv_ref, nb_ref, nm_ref, sems):
    copies = [
        pltpu.make_async_copy(src, dst, sems.at[i])
        for i, (src, dst) in enumerate(((kv_in, kv_ref), (nb_in, nb_ref), (nm_in, nm_ref)))
    ]
    for copy in copies:
        copy.start()
    for copy in copies:
        copy.wait()


def body(tokens, outer_base, outer_momentum, replica_weights, block_exponent):
    rows, depth = tokens.shape
    local, width = outer_base.shape
    dma = pltpu.SemaphoreType.DMA
    vmem = pl.BlockSpec(memory_space=pltpu.VMEM)
    hbm = pl.BlockSpec(memory_space=pltpu.HBM)
    f32, bf16 = jnp.float32, jnp.bfloat16
    step = jax.ShapeDtypeStruct((local, width // NR), f32)
    exponents = jnp.swapaxes(block_exponent, 1, 2)
    operands = (tokens, outer_base, outer_momentum, replica_weights, exponents)
    operands = [pltpu.with_memory_space_constraint(a, pltpu.HBM) for a in operands]
    results = pl.pallas_call(
        kernel,
        out_shape=(jax.ShapeDtypeStruct((rows, width), bf16), step, step),
        in_specs=[hbm] * 5,
        out_specs=(vmem, vmem, vmem),
        scratch_shapes=[
            pltpu.VMEM((rows, depth), bf16),
            pltpu.VMEM((local, width), f32),
            pltpu.VMEM((local, width), f32),
            pltpu.VMEM((1, local, width), bf16),
            pltpu.VMEM(exponents.shape, jnp.int32),
            pltpu.VMEM((8, BLOCK), f32),
            pltpu.VMEM((local, width), bf16),
            pltpu.VMEM((NR, local, width), bf16),
            pltpu.VMEM((NH, NX, NY, 2, local, width), bf16),
            pltpu.VMEM((rows, width), f32),
            dma((5,)),
            dma((NR,)), dma((NR,)),
            dma((7,)), dma((NH,)),
            dma((NH,)), dma((NH, NY)),
            dma((NH,)), dma((NH, NY)), dma((NH, 4)),
            dma((NH,)), dma((NH, NY)),
            dma((NH,)), dma((NH, 4)),
            pltpu.SemaphoreType.REGULAR((7,)),
        ],
        compiler_params=pltpu.CompilerParams(
            collective_id=0, has_side_effects=True, vmem_limit_bytes=32 << 20
        ),
        cost_estimate=pl.CostEstimate(
            flops=2 * rows * depth * width, bytes_accessed=2 * rows * depth, transcendentals=0
        ),
        name="outer_step_project",
    )(*operands)
    results = [pltpu.with_memory_space_constraint(a, pltpu.VMEM) for a in results]
    return pl.pallas_call(
        finish,
        out_shape=tuple(pltpu.HBM(a.shape, a.dtype) for a in results),
        in_specs=[vmem] * 3,
        out_specs=(hbm, hbm, hbm),
        scratch_shapes=[dma((3,))],
        name="write_results",
    )(*results)


def solution(mesh):
    return jax.shard_map(
        body,
        mesh=mesh,
        in_specs=(
            P(("replica", "fsdp"), None),
            P("fsdp", None),
            P("fsdp", None),
            P("replica", "fsdp", None),
            P("replica", "fsdp", None),
        ),
        out_specs=(P(("replica", "fsdp"), None), P("fsdp", "replica"), P("fsdp", "replica")),
        check_vma=False,
    )
```

time: 208 us -> 51.4 us (0.25)
  waiting for transfers between devices: 167 us -> 0 us
  Pallas kernels: 0 us -> 50.6 us
  blocking collectives: 18.5 us -> 0 us
  between operations: 14.1 us -> 0.64 us
  matrix products: 3.81 us -> 0 us
  other arithmetic: 3.19 us -> 0 us
    all_gather x1 -> x0, waiting for transfers between devices: 167 us -> none  [body(): lax.all_gather(weights, 'fsdp', axis=0, tiled=True)]
    pallas_call x0 -> x2, Pallas kernels: none -> 50.6 us  [the longest x1 49.9 us: body(): pl.pallas_call(kernel, out_shape=(jax.ShapeDtypeStruct((rows, width), bf1...]
    psum x1 -> x0, blocking collectives: 18.5 us -> none  [body(): lax.psum(decoded.astype(jnp.bfloat16), 'replica').astype(jnp.float32)]
    dot_general x1 -> x0, matrix products: 3.81 us -> none  [body(): jnp.dot(tokens, lax.all_gather(weights, 'fsdp', axis=0, tiled=True), pref...]
  transfers between devices with their start and end apart: 1 -> 0, of which waited for: 1 -> 0; matrix products, arithmetic and copies ran while one was open for 0% -> 0% of each run, Pallas kernels for 0% -> 0%
where the time goes in v2:
time: 51.4 us; the launch traced here: 51.2 us
  Pallas kernels  50.6 us (98%)
  between operations  0.64 us (1%)
    pallas_call x1, Pallas kernels, body(): pl.pallas_call(kernel, out_shape=(jax.ShapeDtypeStruct((rows, width), bf1...  49.9 us

profile of v2, /device:TPU:1, one launch (start us, length us, event | category | flops | bytes accessed | tf_op | source)
XLA Modules:
  0.0 51.2 jit_solution(13114678122865001535)
XLA Ops:
  0.6 49.9 %outer_step_project.1 = (bf16[192,256]{1,0:T(8,128)(2,1)S(1)}, f32[32,64]{1,0:T(8,128)S(1)}, f32[32,64]{1,0:T(8,128)S(1)}) custom-call(bf16[192,8192]{1,0:T(8,128)(2,1)} %tok_hbm.1, f32[32,256]{1,0:T(8,128)} %base_hbm.1, f32[32,256]{1,0:T(8,128)} %mom_hbm.1, bf16[1,32,256]{2,1,0:T(8,128)(2,1)} %rep_hbm.1, s32[1,2,32]{2,1,0:T(2,128)} %bitcast.1), custom_call_target="tpu_custom_call" | custom-call | flops 805306368 | bytes 3145728 | tf_op jit(solution)/shard_map/outer_step_project/pallas_call | solution.py:335
  50.5 0.7 %write_results.1 = (bf16[192,256]{1,0:T(8,128)(2,1)}, f32[32,64]{1,0:T(8,128)}, f32[32,64]{1,0:T(8,128)}) custom-call(bf16[192,256]{1,0:T(8,128)(2,1)S(1)} %get-tuple-element.6.kv_in, f32[32,64]{1,0:T(8,128)S(1)} %get-tuple-element.7.nb_in, f32[32,64]{1,0:T(8,128)S(1)} %get-tuple-element.8.nm_in), custom_call_target="tpu_custom_call" | custom-call | tf_op jit(solution)/shard_map/write_results/pallas_call | solution.py:369

commit v3 on v2

--- a/solution.py
+++ b/solution.py
@@ -19,16 +19,20 @@
 
 def place():
     r, f = lax.axis_index("replica"), lax.axis_index("fsdp")
-    c, y = f % 2, (f // 2) % NY
-    x, zh = (f // (2 * NY)) % NX, f // (2 * NY * NX)
+    c, y = lax.rem(f, 2), lax.rem(lax.div(f, 2), NY)
+    x, zh = lax.rem(lax.div(f, 2 * NY), NX), lax.div(f, 2 * NY * NX)
     return x, y, zh, r, c
+
+
+def wrap(i, n):
+    return jnp.where(i >= n, i - n, i)
 
 
 def kernel(
     tok_hbm, base_hbm, mom_hbm, rep_hbm, exp_hbm,
     kv_ref, nb_ref, nm_ref,
     tok, base_ref, mom_ref, rep_ref, exp_ref, turn, dec, part, w, acc,
-    in_sem, s0, r0, sh, rh, s1, r1, s3, r3, rest3, s4, r4, sc, rc, ready,
+    in_sem, s0, r0, sh, rh, s1, r1, s3, r3, s4, r4, sc, rc, ready,
 ):
     x, y, zh, r, c = place()
     z = zh * NR + r
@@ -38,16 +42,16 @@
         return (r, ((zh * NX + x) * NY + y) * 2 + c)
 
     def to_r(d):
-        return dev(x, y, zh, (r + d) % NR, c)
+        return dev(x, y, zh, wrap(r + d, NR), c)
 
     def to_y(d):
-        return dev(x, (y + d) % NY, zh, r, c)
+        return dev(x, wrap(y + d, NY), zh, r, c)
 
     def to_x(d):
-        return dev((x + d) % NX, y, zh, r, c)
+        return dev(wrap(x + d, NX), y, zh, r, c)
 
     def at_z(z):
-        return dev(x, y, z // NR, z % NR, c)
+        return dev(x, y, lax.div(z, NR), lax.rem(z, NR), c)
 
     other = dev(x, y, zh, r, 1 - c)
 
@@ -67,9 +71,9 @@
     way = jnp.where(r == 0, -1, 1)
 
     def target(o):
-        return (z + way * o + nz) % nz
-
-    low, high, far = (zh + NH - 1) % NH, (zh + 1) % NH, (zh + 2) % NH
+        return lax.rem(z + way * o + nz, nz)
+
+    low, high, far = wrap(zh + NH - 1, NH), wrap(zh + 1, NH), wrap(zh + 2, NH)
     upward = r < 2
     sources = (
         (low, low * NR + NR - 1, r + 1),
@@ -86,7 +90,7 @@
         pl.when(h > zh)(functools.partial(signal, bar, at_z(src)))
     slots = range(1, 7)
     for o in slots:
-        pl.when(edge & (target(o) // NR > zh))(functools.partial(signal, bar, at_z(target(o))))
+        pl.when(edge & (lax.div(target(o), NR) > zh))(functools.partial(signal, bar, at_z(target(o))))
 
     for load in loads[:4]:
         load.wait()
@@ -109,7 +113,7 @@
         code = code.astype(jnp.bfloat16).astype(jnp.float32)
         dec[:, cols] = (code * down[:, v : v + 1]).astype(jnp.bfloat16)
 
-    below = sum((edge & (target(o) // NR < zh)).astype(jnp.int32) for o in slots)
+    below = sum((edge & (lax.div(target(o), NR) < zh)).astype(jnp.int32) for o in slots)
     below += sum((h < zh).astype(jnp.int32) for h, _, _ in sources)
     pl.semaphore_wait(bar, len(inside) + below)
 
@@ -138,14 +142,14 @@
     average = total / NR
     new_mom = MOMENTUM_RATE * mom_ref[...] + average
     new_base = base_ref[...] - OUTER_RATE * (average + MOMENTUM_RATE * new_mom)
-    own = w.at[zh, x, y, c]
+    own = w.at[c, zh, x, y]
     own[...] = new_base.astype(jnp.bfloat16)
 
     across = NH - 1 - zh
-    order = (zh, zh + 1 - 2 * (zh % 2), across, across + 1 - 2 * (across % 2))
+    order = (zh, zh + 1 - 2 * lax.rem(zh, 2), across, across + 1 - 2 * lax.rem(across, 2))
 
     def push(o, higher):
-        run = target(o) // NR
+        run = lax.div(target(o), NR)
 
         @pl.when(edge & ((run > zh) if higher else (run < zh)))
         def _():
@@ -157,77 +161,73 @@
         for o in (4, 3, 2, 1, 6, 5):
             push(o, True)
 
-    def cell(k, dx, e):
-        return w.at[order[k], (x + dx) % NX, (y + e) % NY, c]
-
-    near = (1, 7, 2, 6, 3, 5, 4)
-    from_left, from_right = (0, 7, 6, 5), (1, 2, 3, 4)
-
-    def x_send(k, e):
-        mine = cell(k, 0, e)
-        for d in (1, 3):
-            on = from_left if d == 1 else from_right
-            sem = r3.at[k, e] if e in on else rest3.at[k, 4 - d]
-            send(mine, s3.at[k], sem, to_x(d))
+    pair = lax.div(y, 2)
+    first = [2 * wrap(pair + j, NY // 2) for j in range(NY // 2)]
+    column = [wrap(x + d, NX) for d in range(NX)]
+    left_x, right_x, up_y = to_x(3), to_x(1), [to_y(e) for e in range(NY)]
+    from_left = (0, 3)
+
+    def cells(k, d, j):
+        return w.at[c, order[k], column[d], pl.ds(first[j], 2)]
 
     def launch(k):
+        mine = w.at[c, order[k], x, y]
         if k > 0:
-            arrive(cell(k, 0, 0), rh.at[order[k]])
-        mine = cell(k, 0, 0)
+            arrive(mine, rh.at[order[k]])
         for e in (4, 3, 5, 2, 6, 1, 7):
-            send(mine, s1.at[k], r1.at[k, NY - e], to_y(e))
-        x_send(k, 0)
-
-    def take(k, e):
-        arrive(cell(k, 0, e), r1.at[k, e])
-        x_send(k, e)
-
-    def forward(k, e):
-        d = 3 if e in from_left else 1
-        block = cell(k, d, e)
-        arrive(block, r3.at[k, e])
-        send(block, s4.at[k], r4.at[k, e], to_x(4 - d))
+            there = wrap(pair + NY // 2 - lax.div(wrap(y + e, NY), 2), NY // 2)
+            send(mine, s1.at[k], r1.at[k, there], up_y[e])
+
+    def take(k, j):
+        mine = cells(k, 0, j)
+        arrive(mine.at[pl.ds(0, 1)] if j == 0 else mine, r1.at[k, j])
+        on = j in from_left
+        send(mine, s3.at[k], r3.at[k, j if on else 4], right_x)
+        send(mine, s3.at[k], r3.at[k, 5 if on else j], left_x)
+
+    def forward(k, j):
+        on = j in from_left
+        block = cells(k, 3 if on else 1, j)
+        arrive(block, r3.at[k, j])
+        send(block, s4.at[k], r4.at[k, j], right_x if on else left_x)
 
     def core_send(k, block, i):
         send(block, sc.at[k], rc.at[k, i], other)
 
     def own_block(k):
-        core_send(k, w.at[order[k], x, :, c], 0)
+        core_send(k, w.at[c, order[k], x], 0)
 
     def side_block(k, d):
-        block = w.at[order[k], (x + d) % NX, :, c]
-        arrive(block.at[pl.ds(0, 4)], rest3.at[k, d])
+        block = w.at[c, order[k], column[d]]
+        arrive(block.at[pl.ds(0, 4)], r3.at[k, 4 if d == 3 else 5])
         core_send(k, block, d)
 
-    def far_cell(k, e):
-        block = cell(k, 2, e)
-        arrive(block, r4.at[k, e])
-        core_send(k, block, 2)
+    def far_cells(k):
+        for j in (0, 1, 3, 2):
+            block = cells(k, 2, j)
+            arrive(block, r4.at[k, j])
+            core_send(k, block, 2)
 
     o = 1 - c
-    depth = NY * 64
+    depth, width = NY * 2 * w.shape[-2], w.shape[-1]
 
     def dot(h, xx):
         at = pl.multiple_of((h * NX + xx) * depth, depth)
-        weights = w[h, xx].reshape(depth, weights_width)
+        weights = jnp.concatenate([w[cc, h, xx, yy] for yy in range(NY) for cc in range(2)], axis=0)
         acc[...] += jnp.dot(tok[:, pl.ds(at, depth)], weights, preferred_element_type=jnp.float32)
-
-    weights_width = w.shape[-1]
 
     def multiply(k):
         h = order[k]
         for d in (0, 3, 1):
-            arrive(w.at[h, (x + d) % NX, :, o], rc.at[k, d])
+            arrive(w.at[o, h, column[d]], rc.at[k, d])
 
         @pl.loop(0, 3)
         def _(i):
-            dot(h, (x + NX - 1 + i) % NX)
+            dot(h, lax.rem(x + NX - 1 + i, NX))
 
     def multiply_far(k):
-        h = order[k]
-        xx = (x + 2) % NX
-        arrive(w.at[h, xx, :, o], rc.at[k, 2])
-        dot(h, xx)
+        arrive(w.at[o, order[k], column[2]], rc.at[k, 2])
+        dot(order[k], column[2])
 
     def write_step():
         for q in range(NR):
@@ -241,51 +241,48 @@
         acc[...] = jnp.zeros_like(acc)
 
     def drain(k):
-        left(w.at[0, 0, pl.ds(0, 7), 0], s1.at[k])
-        left(w.at[0, 0], s3.at[k])
-        left(w.at[0, 0, :, 0], s4.at[k])
-        left(w.at[0, :, :, 0], sc.at[k])
-
-    forwards = (0, 1, 7, 2, 6, 3, 5, 4)
-
+        left(w.at[0, 0, 0, pl.ds(0, 7)], s1.at[k])
+        left(w.at[0, 0, pl.ds(0, 2)], s3.at[k])
+        left(w.at[0, 0, 0], s4.at[k])
+        left(w.at[0, 0], sc.at[k])
+
+    near = (0, 1, 3, 2)
     for o_ in (4, 3, 2, 1, 6, 5):
         push(o_, False)
     launch(0)
     pl.when(zh > 0)(push_up)
     write_step()
-    for e in near:
-        take(0, e)
-    for e in forwards:
-        forward(0, e)
+    for j in near:
+        take(0, j)
+    for j in near:
+        forward(0, j)
     pl.when(zh == 0)(push_up)
     launch(1)
     own_block(0)
     side_block(0, 3)
     side_block(0, 1)
-    for e in near:
-        take(1, e)
+    for j in near:
+        take(1, j)
     loads[4].wait()
-    for e in forwards:
-        far_cell(0, e)
+    far_cells(0)
     multiply(0)
     launch(2)
     launch(3)
-    for e in forwards:
-        forward(1, e)
+    for j in near:
+        forward(1, j)
     own_block(1)
     side_block(1, 3)
     side_block(1, 1)
     multiply_far(0)
-    for e in near:
-        take(2, e)
-        take(3, e)
-    for e in forwards:
-        far_cell(1, e)
+    for j in near:
+        take(2, j)
+        take(3, j)
+    far_cells(1)
     own_block(2)
     own_block(3)
-    for e in forwards:
-        forward(2, e)
-        forward(3, e)
+    for j in near:
+        forward(2, j)
+        forward(3, j)
     side_block(2, 3)
     side_block(2, 1)
     side_block(3, 3)
@@ -294,9 +291,8 @@
     multiply_far(1)
     drain(0)
     drain(1)
-    for e in forwards:
-        far_cell(2, e)
-        far_cell(3, e)
+    far_cells(2)
+    far_cells(3)
     multiply(2)
     multiply(3)
     multiply_far(2)
@@ -346,14 +342,14 @@
             pltpu.VMEM((8, BLOCK), f32),
             pltpu.VMEM((local, width), bf16),
             pltpu.VMEM((NR, local, width), bf16),
-            pltpu.VMEM((NH, NX, NY, 2, local, width), bf16),
+            pltpu.VMEM((2, NH, NX, NY, local, width), bf16),
             pltpu.VMEM((rows, width), f32),
             dma((5,)),
             dma((NR,)), dma((NR,)),
             dma((7,)), dma((NH,)),
-            dma((NH,)), dma((NH, NY)),
-            dma((NH,)), dma((NH, NY)), dma((NH, 4)),
-            dma((NH,)), dma((NH, NY)),
+            dma((NH,)), dma((NH, 4)),
+            dma((NH,)), dma((NH, 6)),
+            dma((NH,)), dma((NH, 4)),
             dma((NH,)), dma((NH, 4)),
             pltpu.SemaphoreType.REGULAR((7,)),
         ],

time: 51.4 us -> 50.5 us (0.982)
  Pallas kernels: 50.6 us -> 49.7 us
    pallas_call x1, Pallas kernels: 49.9 us -> 49 us  [body(): pl.pallas_call(kernel, out_shape=(jax.ShapeDtypeStruct((rows, width), bf1...]
where the time goes in v3:
time: 50.5 us; the launch traced here: 50.3 us
  Pallas kernels  49.7 us (98%)
  between operations  0.64 us (1%)
    pallas_call x1, Pallas kernels, body(): pl.pallas_call(kernel, out_shape=(jax.ShapeDtypeStruct((rows, width), bf1...  49 us

profile of v3, /device:TPU:1, one launch (start us, length us, event | category | flops | bytes accessed | tf_op | source)
XLA Modules:
  0.0 50.3 jit_solution(2034239988295602814)
XLA Ops:
  0.6 49.0 %outer_step_project.1 = (bf16[192,256]{1,0:T(8,128)(2,1)S(1)}, f32[32,64]{1,0:T(8,128)S(1)}, f32[32,64]{1,0:T(8,128)S(1)}) custom-call(bf16[192,8192]{1,0:T(8,128)(2,1)} %tok_hbm.1, f32[32,256]{1,0:T(8,128)} %base_hbm.1, f32[32,256]{1,0:T(8,128)} %mom_hbm.1, bf16[1,32,256]{2,1,0:T(8,128)(2,1)} %rep_hbm.1, s32[1,2,32]{2,1,0:T(2,128)} %bitcast.1), custom_call_target="tpu_custom_call" | custom-call | flops 805306368 | bytes 3145728 | tf_op jit(solution)/shard_map/outer_step_project/pallas_call | solution.py:331
  49.6 0.7 %write_results.1 = (bf16[192,256]{1,0:T(8,128)(2,1)}, f32[32,64]{1,0:T(8,128)}, f32[32,64]{1,0:T(8,128)}) custom-call(bf16[192,256]{1,0:T(8,128)(2,1)S(1)} %get-tuple-element.6.kv_in, f32[32,64]{1,0:T(8,128)S(1)} %get-tuple-element.7.nb_in, f32[32,64]{1,0:T(8,128)S(1)} %get-tuple-element.8.nm_in), custom_call_target="tpu_custom_call" | custom-call | tf_op jit(solution)/shard_map/write_results/pallas_call | solution.py:365
